TPU v7x, 512 devices: a whole 4x4x16 slice. The times are simulated.
512 devices in a mesh: rows: 32 (over z, core), bal: 16 (over x, y).
Axes of the slice: x: 4, y: 4, z: 16, core: 2. Of those that a mesh axis runs over, the one named last changes fastest.
Arguments:
- rhs: float32 [1024, 256], P(('rows', 'bal'))
- self_term: float32 [1024, 256], P(('rows', 'bal')), may hold values from 2.5 to 6
- near_dense_blocks: bfloat16 [4096, 256, 256], P(('rows', 'bal')), may hold values from -0.125 to 0.125
- near_row: int32 [4096], P(('rows', 'bal')), may hold values from 0 to 1023, as said below
- near_column_cluster: int32 [4096], P(('rows', 'bal')), may hold values from 0 to 1023, as said below
- far_left: bfloat16 [3072, 32, 256], P(('rows', 'bal')), may hold values from -0.4375 to 0.4375
- far_right: bfloat16 [3072, 32, 256], P(('rows', 'bal')), may hold values from -0.375 to 0.375
- far_row: int32 [3072], P(('rows', 'bal')), may hold values from 0 to 1023, as said below
- far_col: int32 [3072], P(('rows', 'bal')), may hold values from 0 to 1023
- far_rank: int32 [3072], P(('rows', 'bal')), may hold values from 8 to 32
Outputs:
- solution: float32 [1024, 256], P(('rows', 'bal'))
- next_basis: float32 [1024, 256], P(('rows', 'bal'))
Inputs may be any that keep to these rules, and one draw needn't show every extreme that they name: `near_row`: the row cluster of every near block lies among the 32 row clusters of the index of rows that holds the block. `near_column_cluster`: the column cluster of a near block is at most 3 clusters away from its row cluster, cyclically. `far_row`: the row cluster of every far block lies among the 32 row clusters of the index of rows that holds the block.
All inputs are finite; a program needn't handle non-finite values.
Results may differ from a plain program's by a relative error of at most 0.0163.
Values may be sent and summed in bfloat16 or wider, within the bound.
A program may use at most 64 MiB of HBM per device.

v0:
```python
import jax
import jax.numpy as jnp
from jax import lax
from jax.sharding import PartitionSpec as P


def solve_small(beta, h11, h21, h12, h22, h32):
    radius = jnp.sqrt(h11 * h11 + h21 * h21)
    cosine = h11 / radius
    sine = h21 / radius
    upper = cosine * h12 + sine * h22
    lower = cosine * h22 - sine * h12
    radius_two = jnp.sqrt(lower * lower + h32 * h32)
    coef_two = -(lower / radius_two) * sine * beta / radius_two
    coef_one = (cosine * beta - upper * coef_two) / radius
    return (coef_one, coef_two)


def projection_sum(first, second):
    return lax.psum(jnp.sum(first * second), ("rows", "bal"))


def length_sum(vector):
    return lax.psum(jnp.sum(vector * vector), ("rows", "bal"))


def shards(
    rhs,
    self_term,
    near_dense_blocks,
    near_row,
    near_column_cluster,
    far_left,
    far_right,
    far_row,
    far_col,
    far_rank,
):
    cl_count = rhs.shape[0]
    group_size = cl_count * lax.axis_size("bal")
    base = lax.axis_index("rows") * group_size
    rank_width = far_left.shape[1]
    near_select = (
        lax.broadcasted_iota(jnp.int32, (group_size, near_row.shape[0]), 0)
        == (near_row - base)[None, :]
    ).astype(jnp.float32)
    far_select = (
        lax.broadcasted_iota(jnp.int32, (group_size, far_row.shape[0]), 0)
        == (far_row - base)[None, :]
    ).astype(jnp.float32)
    keep = jnp.arange(rank_width, dtype=jnp.int32)[None, :] < far_rank[:, None]

    def operate(vec):
        source = vec.astype(jnp.bfloat16)
        whole = lax.all_gather(source, ("rows", "bal"), axis=0, tiled=True)
        picked = whole[near_column_cluster]
        near_contributions = jnp.einsum(
            "kij,kj->ki", near_dense_blocks, picked, preferred_element_type=jnp.float32
        )
        far_picked = whole[far_col]
        coeff = jnp.einsum("krj,kj->kr", far_right, far_picked, preferred_element_type=jnp.float32)
        coeff = jnp.where(keep, coeff, 0.0).astype(jnp.bfloat16)
        far_terms = jnp.einsum("krj,kr->kj", far_left, coeff, preferred_element_type=jnp.float32)
        partial_rows = jnp.dot(near_select, near_contributions, precision=lax.Precision.HIGHEST)
        partial_rows = partial_rows + jnp.dot(
            far_select, far_terms, precision=lax.Precision.HIGHEST
        )
        summed = lax.psum_scatter(
            partial_rows.astype(jnp.bfloat16), "bal", scatter_dimension=0, tiled=True
        ).astype(jnp.float32)
        return self_term * vec + summed

    beta = jnp.sqrt(lax.psum(jnp.sum(rhs * rhs), ("rows", "bal")))
    first = rhs / beta
    image = operate(first)
    h11 = projection_sum(first, image)
    remain = image - h11 * first
    h21 = jnp.sqrt(length_sum(remain) + 1e-06)
    second = remain / h21
    image = operate(second)
    h12 = projection_sum(first, image)
    remain = image - h12 * first
    h22 = projection_sum(second, remain)
    remain = remain - h22 * second
    h32 = jnp.sqrt(length_sum(remain) + 1e-06)
    next_basis = remain / h32
    coef_one, coef_two = solve_small(beta, h11, h21, h12, h22, h32)
    solution = coef_one * first + coef_two * second
    return (solution, next_basis)


def solution(mesh):
    in_specs = (
        P(("rows", "bal"), None),
        P(("rows", "bal"), None),
        P(("rows", "bal"), None, None),
        P(("rows", "bal")),
        P(("rows", "bal")),
        P(("rows", "bal"), None, None),
        P(("rows", "bal"), None, None),
        P(("rows", "bal")),
        P(("rows", "bal")),
        P(("rows", "bal")),
    )
    out_specs = (P(("rows", "bal"), None), P(("rows", "bal"), None))
    return jax.shard_map(shards, mesh=mesh, in_specs=in_specs, out_specs=out_specs, check_vma=False)
```

profile of v0, /device:TPU:1, one launch (start us, length us, event | category | flops | bytes accessed | tf_op | source)
XLA Modules:
  0.0 1161.6 jit_solution(9268671512109086192)
XLA Ops:
  0.6 1.4 multiply_reduce_fusion.5
  2.0 111.0 %psum.42 = f32[]{:T(128)} all-reduce(f32[]{:T(128)} %multiply_reduce_fusion.5), channel_id=1, replica_groups=mesh['rows'=32,'bal'=16] {'rows','bal'}, use_global_device_ids=true, to_apply=%region_1.0 | all-reduce | flops 1 | bytes 8 | tf_op jit(solution)/shard_map/psum | solution.py:73
  113.7 192.6 %all-gather = bf16[512,2,256]{2,1,0:T(2,128)(2,1)S(1)} all-gather(bf16[1,2,256]{2,1,0:T(2,128)(2,1)S(1)} %get-tuple-element.8), channel_id=1, replica_groups=mesh['rows'=32,'bal'=16] {'rows','bal'}, dimensions={0}, use_global_device_ids=true | all-gather | bytes 525312 | tf_op jit(solution)/shard_map/all_gather | solution.py:55
  307.0 0.6 gather_fusion
  308.4 0.6 gather_fusion.1
  309.1 0.5 copy-done.4
  309.9 0.5 copy-done.9
  310.5 57.9 %all-reduce = bf16[32,256]{1,0:T(8,128)(2,1)S(1)} all-reduce(bf16[32,256]{1,0:T(8,128)(2,1)S(1)} %fusion), channel_id=2, replica_groups=mesh['rows'=32,'bal'=16] {'bal'}, use_global_device_ids=true, to_apply=%region_2.3.clone | all-reduce | flops 8192 | bytes 32768
  368.4 1.3 dynamic-slice
  370.4 0.6 multiply_reduce_fusion.4
  371.0 112.3 %psum.43 = f32[]{:T(128)} all-reduce(f32[]{:T(128)} %multiply_reduce_fusion.4), channel_id=1, replica_groups=mesh['rows'=32,'bal'=16] {'rows','bal'}, use_global_device_ids=true, to_apply=%region_4.5 | all-reduce | flops 1 | bytes 8 | tf_op jit(solution)/shard_map/psum | solution.py:20
  483.2 1.3 multiply_reduce_fusion.3
  484.5 100.4 %psum.44 = f32[]{:T(128)} all-reduce(f32[]{:T(128)} %get-tuple-element.6), channel_id=1, replica_groups=mesh['rows'=32,'bal'=16] {'rows','bal'}, use_global_device_ids=true, to_apply=%region_6.7 | all-reduce | flops 1 | bytes 8 | tf_op jit(solution)/shard_map/psum | solution.py:24
  587.6 194.7 %all-gather.1 = bf16[512,2,256]{2,1,0:T(2,128)(2,1)S(1)} all-gather(bf16[1,2,256]{2,1,0:T(2,128)(2,1)S(1)} %get-tuple-element.4), channel_id=1, replica_groups=mesh['rows'=32,'bal'=16] {'rows','bal'}, dimensions={0}, use_global_device_ids=true | all-gather | bytes 525312 | tf_op jit(solution)/shard_map/all_gather | solution.py:55
  782.5 0.6 gather_fusion.2
  783.6 0.6 gather_fusion.3
  784.6 57.9 %all-reduce.1 = bf16[32,256]{1,0:T(8,128)(2,1)S(1)} all-reduce(bf16[32,256]{1,0:T(8,128)(2,1)S(1)} %fusion.1), channel_id=3, replica_groups=mesh['rows'=32,'bal'=16] {'bal'}, use_global_device_ids=true, to_apply=%region_7.8.clone | all-reduce | flops 8192 | bytes 32768
  842.5 0.6 multiply_reduce_fusion.2
  843.1 111.3 %psum.45 = f32[]{:T(128)} all-reduce(f32[]{:T(128)} %multiply_reduce_fusion.2), channel_id=1, replica_groups=mesh['rows'=32,'bal'=16] {'rows','bal'}, use_global_device_ids=true, to_apply=%region_9.10 | all-reduce | flops 1 | bytes 8 | tf_op jit(solution)/shard_map/psum | solution.py:20
  954.5 1.3 multiply_reduce_fusion.1
  955.7 100.4 %psum.46 = f32[]{:T(128)} all-reduce(f32[]{:T(128)} %multiply_reduce_fusion.1), channel_id=1, replica_groups=mesh['rows'=32,'bal'=16] {'rows','bal'}, use_global_device_ids=true, to_apply=%region_11.12 | all-reduce | flops 1 | bytes 8 | tf_op jit(solution)/shard_map/psum | solution.py:20
  1057.4 2.0 multiply_reduce_fusion
  1059.4 99.5 %psum.47 = f32[]{:T(128)} all-reduce(f32[]{:T(128)} %get-tuple-element.2), channel_id=1, replica_groups=mesh['rows'=32,'bal'=16] {'rows','bal'}, use_global_device_ids=true, to_apply=%region_13.14 | all-reduce | flops 1 | bytes 8 | tf_op jit(solution)/shard_map/psum | solution.py:24
  1161.0 0.6 multiply_add_fusion
  (40 shorter events, 3.2 us)
Async XLA Ops:
  0.6 306.9 %copy-start = (bf16[8,256,256]{2,1,0:T(8,128)(2,1)S(1)}, bf16[8,256,256]{2,1,0:T(8,128)(2,1)}, u32[]{:S(2)}) copy-start(bf16[8,256,256]{2,1,0:T(8,128)(2,1)} %param.12) | copy-start | bytes 3145732
  2.0 111.7 %copy-start.3 = (f32[2,256]{1,0:T(2,128)S(1)}, f32[2,256]{1,0:T(2,128)}, u32[]{:S(2)}) copy-start(f32[2,256]{1,0:T(2,128)} %param.10) | copy-start | bytes 6148
  306.3 0.7 copy-start.6
  307.6 0.7 copy-start.7
  307.6 0.8 copy-start.8
  308.0 1.0 copy-start.5
  308.2 1.5 copy-start.1
  309.0 0.7 copy-start.4
  309.7 0.7 copy-start.9
  369.7 0.7 copy-start.2
where the time goes:
time: 1160 us
  blocking collectives  1140 us (98%)
    all_gather x2, blocking collectives, operate(): whole = lax.all_gather(source, ('rows', 'bal'), axis=0, tiled=True)  387 us
    psum x3, blocking collectives, projection_sum(): return lax.psum(jnp.sum(first * second), ('rows', 'bal'))  324 us
    psum x2, blocking collectives, length_sum(): return lax.psum(jnp.sum(vector * vector), ('rows', 'bal'))  200 us
    unnamed x2, blocking collectives  116 us
    psum x1, blocking collectives, shards(): beta = jnp.sqrt(lax.psum(jnp.sum(rhs * rhs), ('rows', 'bal')))  111 us

commit v1 on v0

v1 whole, which is shorter than its diff:
```python
import jax
import jax.numpy as jnp
from jax import lax
from jax.experimental import pallas as pl
from jax.experimental.pallas import tpu as pltpu
from jax.sharding import PartitionSpec as P

MESH = pl.DeviceIdType.MESH
F32 = jnp.float32
BF16 = jnp.bfloat16
NEAR, FARS, RANK = 8, 6, 32

RING_HOPS = (0, 1, 2, 1)
PLANE = sorted(range(1, 16), key=lambda j: -(RING_HOPS[j // 4] + RING_HOPS[j % 4]))
ALONG = sorted(range(1, 16), key=lambda i: -min(i, 16 - i))
SLOT = {i: (4 - i) % 16 for i in range(16)}
OFFSETS = ((0, 12), (4, 8))


def total(value):
    return jnp.sum(jnp.sum(value, axis=0, keepdims=True), axis=1, keepdims=True)


def kernel(
    near_row, near_col, far_row, far_col, far_rank,
    rhs, self_term, near_hbm, left_hbm, right_hbm,
    solution_out, basis_out,
    near, left, right, load_sem,
    own, along, along_send, along_recv,
    plane, plane_send, plane_recv,
    whole, gather_send, gather_recv, core_send, core_recv,
    terms, terms_send, terms_recv,
    tile, tile_send, tile_recv,
    sums, sums_send, sums_recv, pair, pair_send, pair_recv,
    hot, flat_rhs, flat_self, flat_along, pick,
):
    r = lax.axis_index("rows")
    b = lax.axis_index("bal")
    z, c = r // 2, r % 2
    x, y = b // 4, b % 4

    def along_z(i):
        return (((z + i + 16) % 16) * 2 + c, b)

    def in_plane(j):
        jx, jy = j // 4, j % 4
        px = x + jx - 2 * (x % 2) * (jx % 2) - 4 * ((x // 2) * (jx // 2))
        py = y + jy - 2 * (y % 2) * (jy % 2) - 4 * ((y // 2) * (jy // 2))
        return px * 4 + py

    sibling = (z * 2 + 1 - c, b)
    peer = {j: in_plane(j) for j in PLANE}

    barrier = pltpu.get_barrier_semaphore()
    for i in ALONG:
        pl.semaphore_signal(barrier, inc=1, device_id=along_z(i), device_id_type=MESH)
    for j in PLANE:
        pl.semaphore_signal(barrier, inc=1, device_id=(r, peer[j]), device_id_type=MESH)
    pl.semaphore_signal(barrier, inc=1, device_id=sibling, device_id_type=MESH)

    loads = [
        pltpu.make_async_copy(a, v, load_sem.at[n])
        for n, (a, v) in enumerate(((near_hbm, near), (left_hbm, left), (right_hbm, right)))
    ]
    for load in loads:
        load.start()

    def halves(value):
        return jnp.concatenate([value[:, :128], value[:, 128:]], axis=0)

    own_rhs = halves(rhs[...])
    own[...] = own_rhs
    along[4] = own_rhs

    base = r * 32
    lane = lax.broadcasted_iota(jnp.int32, (4, 128), 0) * 128 + lax.broadcasted_iota(jnp.int32, (4, 128), 1)
    mine = (lane // 16) % 16 == b
    half_of = (lane // 8) % 2
    task_of = lane % 8 + 8 * (lane // 256)
    row_of = jnp.full((4, 128), -1, jnp.int32)
    for k in range(NEAR + FARS):
        local = (near_row[k] if k < NEAR else far_row[k - NEAR]) - base
        row_of = jnp.where(mine & (task_of == k), 2 * local - local % 2, row_of)
    place = jnp.where(row_of >= 0, row_of + 2 * half_of + 1, 0).astype(F32)
    plane[b] = jnp.concatenate([own_rhs, halves(self_term[...]), place, jnp.zeros((4, 128), F32)], axis=0)

    pl.semaphore_wait(barrier, 31)

    pending = []

    def send(src, dst, send_sem, recv_sem, device):
        copy = pltpu.make_async_remote_copy(
            src_ref=src, dst_ref=dst, send_sem=send_sem, recv_sem=recv_sem, device_id=device, device_id_type=MESH
        )
        copy.start()
        pending.append(copy)

    def arrived(dst, recv_sem):
        pltpu.make_async_remote_copy(
            src_ref=dst, dst_ref=dst, send_sem=recv_sem, recv_sem=recv_sem, device_id=sibling, device_id_type=MESH
        ).wait_recv()

    for i in ALONG:
        send(own, along.at[SLOT[i]], along_send.at[i], along_recv.at[SLOT[i]], along_z(i))
    for j in PLANE:
        send(plane.at[b], plane.at[b], plane_send.at[j], plane_recv.at[j], (r, peer[j]))

    task = lax.broadcasted_iota(jnp.int32, (32, 1), 0)
    half = task // 16
    place_1 = jnp.full((32, 1), -1, jnp.int32)
    place_2 = jnp.full((32, 1), -1, jnp.int32)
    for k in range(NEAR + FARS):
        col = near_col[k] if k < NEAR else far_col[k - NEAR]
        other = jnp.where((col // 32) % 2 == c, 0, 1)
        d = (col // 64 - z + 16) % 16
        dev = (col % 32) // 2
        cl = col % 2
        e = (d + 4) % 16
        p1 = (((other * 2 + e // 8) * 16 + dev) * 2 + (e // 4) % 2) * 16 + (e % 4) * 4 + cl
        m = d // 4
        batch = jnp.where((m == 1) | (m == 2), 1, 0)
        holder = (d % 4) * 4 + dev // 4
        p2 = (((other * 2 + batch) * 16 + holder) * 2 + m // 2) * 16 + (dev % 4) * 4 + cl
        place_1 = jnp.where(task % 16 == k, p1 + 2 * half, place_1)
        place_2 = jnp.where(task % 16 == k, p2 + 2 * half, place_2)
    spot = lax.broadcasted_iota(jnp.int32, (32, 512), 1)
    for g in range(4):
        hot[0, g] = jnp.where(spot + 512 * g == place_1, 1.0, 0.0).astype(BF16)
        hot[1, g] = jnp.where(spot + 512 * g == place_2, 1.0, 0.0).astype(BF16)

    rank_of = jnp.zeros((16, 1), jnp.int32)
    task16 = lax.broadcasted_iota(jnp.int32, (16, 1), 0)
    for k in range(FARS):
        rank_of = jnp.where(task16 == NEAR + k, far_rank[k], rank_of)
    lane192 = lax.broadcasted_iota(jnp.int32, (16, FARS * RANK), 1)
    keep = (lane192 // RANK + NEAR == task16) & (lane192 % RANK < rank_of)

    def send_batch(it, batch):
        for j in PLANE:
            part = whole.at[it, 0, batch, b]
            send(part, part, gather_send.at[it, batch, j], gather_recv.at[it, batch, j], (r, peer[j]))

    def finish_batch(it, batch):
        for j in PLANE:
            arrived(whole.at[it, 0, batch, peer[j]], gather_recv.at[it, batch, j])
        send(whole.at[it, 0, batch], whole.at[it, 1, batch], core_send.at[it, batch], core_recv.at[it, batch], sibling)

    def picked(it, other, batch):
        source = whole[it, other, batch].reshape(512, 128)
        return jnp.dot(hot[it, other * 2 + batch], source, preferred_element_type=F32)

    def joined(value):
        return jnp.concatenate([value[:16], value[16:]], axis=1)

    def send_terms(it, kind, value):
        terms[it, kind, b] = halves(value).astype(BF16)
        for j in PLANE:
            part = terms.at[it, kind, b]
            send(part, part, terms_send.at[it, kind, j], terms_recv.at[it, kind, j], (r, peer[j]))

    def take_terms(it, kind, select):
        for j in PLANE:
            arrived(terms.at[it, kind, peer[j]], terms_recv.at[it, kind, j])
        return jnp.dot(select, terms[it, kind].reshape(256, 128), preferred_element_type=F32)

    def near_terms(picks):
        source = joined(picks)
        out = jnp.zeros((16, 256), F32)
        for k in range(NEAR):
            one = jnp.where(task16 == k, source, 0.0).astype(BF16)
            out += lax.dot_general(one, near[k], (((1,), (1,)), ((), ())), preferred_element_type=F32)
        return out[:8]

    def far_terms(picks):
        source = joined(picks).astype(BF16)
        coeff = lax.dot_general(
            source, right[...].reshape(FARS * RANK, 256), (((1,), (1,)), ((), ())), preferred_element_type=F32
        )
        coeff = jnp.where(keep, coeff, 0.0).astype(BF16)
        return jnp.dot(coeff, left[...].reshape(FARS * RANK, 256), preferred_element_type=F32)[8:]

    def send_sums(stage, values):
        lanes = lax.broadcasted_iota(jnp.int32, (1, 128), 1)
        row = jnp.zeros((1, 128), F32)
        for n, value in enumerate(values):
            row = jnp.where(lanes == n, value, row)
        sums[stage, z] = row
        for i in ALONG:
            part = sums.at[stage, z]
            send(part, part, sums_send.at[stage, i], sums_recv.at[stage, i], along_z(i))

    def pair_sums(stage):
        for i in ALONG:
            arrived(sums.at[stage, (z - i + 16) % 16], sums_recv.at[stage, i])
        pair[stage, 0] = jnp.sum(sums[stage], axis=0)
        send(pair.at[stage, 0], pair.at[stage, 1], pair_send.at[stage], pair_recv.at[stage], sibling)

    def take_sums(stage, count):
        arrived(pair.at[stage, 1], pair_recv.at[stage])
        row = pair[stage, 0] + pair[stage, 1]
        return [row[:, n : n + 1] for n in range(count)]

    def along_batch(batch):
        for e in range(8 * batch, 8 * batch + 8):
            if e != 4:
                arrived(along.at[e], along_recv.at[e])
            flat_along[4 * e : 4 * e + 4] = along[e]
        part = flat_along[32 * batch : 32 * batch + 32].astype(BF16)
        whole[0, 0, batch, b] = part.reshape(2, 16, 128)
        send_batch(0, batch)

    along_batch(0)
    for j in PLANE:
        arrived(plane.at[peer[j]], plane_recv.at[j])
    index = jnp.zeros((4, 128), F32)
    for dev in range(16):
        flat_rhs[4 * dev : 4 * dev + 4] = plane[dev, 0:4]
        flat_self[4 * dev : 4 * dev + 4] = plane[dev, 4:8]
        index += plane[dev, 8:12]
    index = index.astype(jnp.int32)
    spots = lax.broadcasted_iota(jnp.int32, (64, 256), 0) + 1
    selects = [
        jnp.where(
            spots == jnp.concatenate([index[2 * kind : 2 * kind + 1], index[2 * kind + 1 : 2 * kind + 2]], axis=1),
            1.0, 0.0,
        ).astype(BF16)
        for kind in range(2)
    ]
    squares = flat_rhs[...] * flat_rhs[...]
    send_sums(0, [total(squares), total(squares * flat_self[...])])
    along_batch(1)

    def operate(it, before_far):
        finish_batch(it, 0)
        picks = picked(it, 0, 0)
        arrived(whole.at[it, 1, 0], core_recv.at[it, 0])
        picks += picked(it, 1, 0)
        if it == 0:
            for load in loads:
                load.wait()
        send_terms(it, 0, near_terms(picks))
        pick[...] = picks
        if it == 1:
            before_far()
        finish_batch(it, 1)
        picks = pick[...] + picked(it, 0, 1)
        if it == 0:
            before_far()
        arrived(whole.at[it, 1, 1], core_recv.at[it, 1])
        picks += picked(it, 1, 1)
        send_terms(it, 1, far_terms(picks))
        out = take_terms(it, 0, selects[0])
        return out + take_terms(it, 1, selects[1])

    image = operate(0, lambda: pair_sums(0))
    beta_squared, diagonal = take_sums(0, 2)
    beta = jnp.sqrt(beta_squared)
    guess = diagonal / beta_squared
    first = flat_rhs[...] / beta
    image = (flat_self[...] * flat_rhs[...] + image) / beta
    shifted = image - guess * first

    tile[...] = shifted.astype(BF16).reshape(4, 16, 128)

    def tile_copy(batch, n):
        number = batch * 2 + n
        part = whole.at[1, 0, batch, b, n]
        source = (z - x - OFFSETS[batch][n] + 32) % 16
        return pltpu.make_async_remote_copy(
            src_ref=tile.at[y], dst_ref=part, send_sem=tile_send.at[number], recv_sem=tile_recv.at[number],
            device_id=(source * 2 + c, b), device_id_type=MESH,
        )

    for batch, n in ((1, 1), (1, 0), (0, 1)):
        tile_copy(batch, n).start()

    @pl.when(x > 0)
    def _():
        tile_copy(0, 0).start()

    @pl.when(x == 0)
    def _():
        whole[1, 0, 0, b, 0] = tile[y]

    send_sums(1, [total(first * first), total(first * shifted), total(shifted * shifted)])

    @pl.when(x > 0)
    def _():
        tile_copy(0, 0).wait_recv()

    tile_copy(0, 1).wait_recv()
    send_batch(1, 0)
    tile_copy(1, 0).wait_recv()
    tile_copy(1, 1).wait_recv()
    send_batch(1, 1)

    second = operate(1, lambda: pair_sums(1))
    g11, p1, p2 = take_sums(1, 3)
    h11 = guess * g11 + p1
    step = h11 - guess
    h21 = jnp.sqrt(jnp.maximum(p2 - 2.0 * step * p1 + step * step * g11, 0.0) + 1e-06)
    second = (flat_self[...] * shifted + second - step * image) / h21
    basis = (shifted - step * first) / h21
    rest = second - guess * basis
    send_sums(
        2,
        [total(first * rest), total(basis * rest), total(rest * rest), total(first * basis), total(basis * basis)],
    )

    def mine_of(value):
        flat_along[...] = value
        two = flat_along[pl.ds(pl.multiple_of((b // 2) * 8, 8), 8), :]
        return jnp.where(b % 2 == 0, two[:4], two[4:])

    own_first, own_basis, own_rest = mine_of(first), mine_of(basis), mine_of(rest)

    pair_sums(2)
    q1, q2, q3, g12, g22 = take_sums(2, 5)
    h12 = q1 + guess * g12
    h22 = q2 + guess * g22
    left_over = h22 - guess
    square = (
        q3 - 2.0 * h12 * q1 - 2.0 * left_over * q2
        + h12 * h12 * g11 + left_over * left_over * g22 + 2.0 * h12 * left_over * g12
    )
    h32 = jnp.sqrt(jnp.maximum(square, 0.0) + 1e-06)

    radius = jnp.sqrt(h11 * h11 + h21 * h21)
    cosine = h11 / radius
    sine = h21 / radius
    upper = cosine * h12 + sine * h22
    lower = cosine * h22 - sine * h12
    radius_two = jnp.sqrt(lower * lower + h32 * h32)
    coef_two = -(lower / radius_two) * sine * beta / radius_two
    coef_one = (cosine * beta - upper * coef_two) / radius

    def put(out, value):
        out[...] = jnp.concatenate([value[0:2], value[2:4]], axis=1)

    put(solution_out, coef_one * own_first + coef_two * own_basis)
    put(basis_out, (own_rest - h12 * own_first - left_over * own_basis) / h32)

    for copy in pending:
        copy.wait_send()
    for batch, n in ((1, 1), (1, 0), (0, 1)):
        tile_copy(batch, n).wait_send()

    @pl.when(x > 0)
    def _():
        tile_copy(0, 0).wait_send()


def shards(rhs, self_term, near_blocks, near_row, near_col, far_left, far_right, far_row, far_col, far_rank):
    vmem = pl.BlockSpec(memory_space=pltpu.VMEM)
    smem = pl.BlockSpec(memory_space=pltpu.SMEM)
    anywhere = pl.BlockSpec(memory_space=pl.ANY)
    dma = pltpu.SemaphoreType.DMA
    return pl.pallas_call(
        kernel,
        out_shape=[jax.ShapeDtypeStruct(rhs.shape, F32)] * 2,
        in_specs=[smem] * 5 + [vmem] * 2 + [anywhere] * 3,
        out_specs=[vmem] * 2,
        scratch_shapes=[
            pltpu.VMEM(near_blocks.shape, BF16), pltpu.VMEM(far_left.shape, BF16), pltpu.VMEM(far_right.shape, BF16),
            dma((3,)),
            pltpu.VMEM((4, 128), F32), pltpu.VMEM((16, 4, 128), F32), dma((16,)), dma((16,)),
            pltpu.VMEM((16, 16, 128), F32), dma((16,)), dma((16,)),
            pltpu.VMEM((2, 2, 2, 16, 2, 16, 128), BF16), dma((2, 2, 16)), dma((2, 2, 16)), dma((2, 2)), dma((2, 2)),
            pltpu.VMEM((2, 2, 16, 16, 128), BF16), dma((2, 2, 16)), dma((2, 2, 16)),
            pltpu.VMEM((4, 16, 128), BF16), dma((4,)), dma((4,)),
            pltpu.VMEM((3, 16, 1, 128), F32), dma((3, 16)), dma((3, 16)),
            pltpu.VMEM((3, 2, 1, 128), F32), dma((3,)), dma((3,)),
            pltpu.VMEM((2, 4, 32, 512), BF16), pltpu.VMEM((64, 128), F32), pltpu.VMEM((64, 128), F32),
            pltpu.VMEM((64, 128), F32), pltpu.VMEM((32, 128), F32),
        ],
        compiler_params=pltpu.CompilerParams(
            collective_id=0, has_side_effects=True, vmem_limit_bytes=24 * 1024 * 1024
        ),
        name="gmres",
    )(near_row, near_col, far_row, far_col, far_rank, rhs, self_term, near_blocks, far_left, far_right)


def solution(mesh):
    vec = P(("rows", "bal"), None)
    blocks = P(("rows", "bal"), None, None)
    ints = P(("rows", "bal"))
    in_specs = (vec, vec, blocks, ints, ints, blocks, blocks, ints, ints, ints)
    return jax.shard_map(shards, mesh=mesh, in_specs=in_specs, out_specs=(vec, vec), check_vma=False)
```

time: 1160 us -> 76.2 us (0.07)
  blocking collectives: 1140 us -> 0 us
  Pallas kernels: 0 us -> 66.4 us
    psum x6 -> x0, blocking collectives: 635 us -> none  [the longest x3 324 us: projection_sum(): return lax.psum(jnp.sum(first * second), ('rows', 'bal'))]
    all_gather x2 -> x0, blocking collectives: 387 us -> none  [operate(): whole = lax.all_gather(source, ('rows', 'bal'), axis=0, tiled=True)]
    unnamed x2 -> x0, blocking collectives: 116 us -> none
    pallas_call x0 -> x1, Pallas kernels: none -> 66.4 us  [shards(): pl.pallas_call(kernel, out_shape=[jax.ShapeDtypeStruct(rhs.shape, F32)] *...]
where the time goes in v1:
time: 76.2 us; the launch traced here: 75.8 us
  Pallas kernels  66.4 us (87%)
  local copies, waits for them, and re-layouts  8.8 us (12%)
    pallas_call x1, Pallas kernels, shards(): pl.pallas_call(kernel, out_shape=[jax.ShapeDtypeStruct(rhs.shape, F32)] *...  66.4 us
    unnamed x22, local copies, waits for them, and re-layouts  8.8 us

profile of v1, /device:TPU:1, one launch (start us, length us, event | category | flops | bytes accessed | tf_op | source)
XLA Modules:
  0.0 75.8 jit_solution(18138817872981496785)
XLA Ops:
  0.6 0.0 copy-start
  0.6 1.2 %copy-done = bf16[8,256,256]{2,1,0:T(8,128)(2,1)S(1)} copy-done((bf16[8,256,256]{2,1,0:T(8,128)(2,1)S(1)}, bf16[8,256,256]{2,1,0:T(8,128)(2,1)}, u32[]{:S(2)}) %copy-start) | copy-done | bytes 1048600
  1.9 0.0 copy-start.1
  1.9 0.9 %copy-done.1 = bf16[6,32,256]{2,1,0:T(8,128)(2,1)S(1)} copy-done((bf16[6,32,256]{2,1,0:T(8,128)(2,1)S(1)}, bf16[6,32,256]{2,1,0:T(8,128)(2,1)}, u32[]{:S(2)}) %copy-start.1) | copy-done | bytes 98328
  2.8 0.0 copy-start.2
  2.8 0.9 %copy-done.2 = bf16[6,32,256]{2,1,0:T(8,128)(2,1)S(1)} copy-done((bf16[6,32,256]{2,1,0:T(8,128)(2,1)S(1)}, bf16[6,32,256]{2,1,0:T(8,128)(2,1)}, u32[]{:S(2)}) %copy-start.2) | copy-done | bytes 98328
  3.6 0.0 copy-start.3
  3.6 0.7 copy-done.3
  4.3 0.0 copy-start.4
  4.3 0.7 copy-done.4
  5.0 0.0 copy-start.5
  5.0 0.7 copy-done.5
  5.7 0.0 copy-start.6
  5.7 0.7 copy-done.6
  6.3 0.0 copy-start.7
  6.3 0.7 copy-done.7
  7.0 0.0 copy-start.8
  7.0 0.7 copy-done.8
  7.6 0.0 copy-start.9
  7.6 0.7 copy-done.9
  8.3 66.4 %gmres.1 = (f32[2,256]{1,0:T(2,128)S(1)}, f32[2,256]{1,0:T(2,128)S(1)}) custom-call(s32[8]{0:T(128)S(1)} %copy-done.5, s32[8]{0:T(128)S(1)} %copy-done.6, s32[6]{0:T(128)S(1)} %copy-done.7, s32[6]{0:T(128)S(1)} %copy-done.8, s32[6]{0:T(128)S(1)} %copy-done.9, f32[2,256]{1,0:T(2,128)S(1)} %copy-done.3, f32[2,256]{1,0:T(2,128)S(1)} %copy-done.4, ...), custom_call_target="tpu_custom_call" | custom-call | tf_op jit(solution)/shard_map/gmres/pallas_call | solution.py:358
  74.7 0.6 copy.14
  75.3 0.6 copy.15
Async XLA Ops:
  0.6 1.2 %copy-start = (bf16[8,256,256]{2,1,0:T(8,128)(2,1)S(1)}, bf16[8,256,256]{2,1,0:T(8,128)(2,1)}, u32[]{:S(2)}) copy-start(bf16[8,256,256]{2,1,0:T(8,128)(2,1)} %near_hbm.1) | copy-start | bytes 3145732
  1.9 0.9 %copy-start.1 = (bf16[6,32,256]{2,1,0:T(8,128)(2,1)S(1)}, bf16[6,32,256]{2,1,0:T(8,128)(2,1)}, u32[]{:S(2)}) copy-start(bf16[6,32,256]{2,1,0:T(8,128)(2,1)} %left_hbm.1) | copy-start | bytes 294916
  2.8 0.9 %copy-start.2 = (bf16[6,32,256]{2,1,0:T(8,128)(2,1)S(1)}, bf16[6,32,256]{2,1,0:T(8,128)(2,1)}, u32[]{:S(2)}) copy-start(bf16[6,32,256]{2,1,0:T(8,128)(2,1)} %right_hbm.1) | copy-start | bytes 294916
  3.6 0.7 copy-start.3
  4.3 0.7 copy-start.4
  5.0 0.7 copy-start.5
  5.7 0.7 copy-start.6
  6.3 0.7 copy-start.7
  7.0 0.7 copy-start.8
  7.6 0.7 copy-start.9

commit v2 on v1

v2 whole, which is shorter than its diff:
```python
import jax
import jax.numpy as jnp
from jax import lax
from jax.experimental import pallas as pl
from jax.experimental.pallas import tpu as pltpu
from jax.sharding import PartitionSpec as P

MESH = pl.DeviceIdType.MESH
F32 = jnp.float32
BF16 = jnp.bfloat16
NEAR, FARS, RANK = 8, 6, 32

RING_HOPS = (0, 1, 2, 1)
PLANE = sorted(range(1, 16), key=lambda j: -(RING_HOPS[j // 4] + RING_HOPS[j % 4]))
ALONG = sorted(range(1, 16), key=lambda i: -min(i, 16 - i))


def signed(i):
    return i if i <= 8 else i - 16


def ranked(d):
    return 2 * abs(d) - (d > 0)


RANKS = {i: ranked(signed(-i % 16)) for i in ALONG}
BOUNDS = ((0, 4, 3), (4, 12, 8), (12, 20, 8))


def total(value):
    return jnp.sum(jnp.sum(value, axis=0, keepdims=True), axis=1, keepdims=True)


def kernel(
    near_row_hbm, near_col_hbm, far_row_hbm, far_col_hbm, far_rank_hbm,
    rhs_hbm, self_hbm, near_hbm, left_hbm, right_hbm,
    out,
    near_row, near_col, far_row, far_col, far_rank, rhs, self_term,
    near, left, right, load_sem,
    own, along, along_send, along_recv,
    plane, plane_send, plane_recv,
    first_tiles, middle_tiles, last_tiles, gather_send, gather_recv, core_send, core_recv,
    terms, terms_send, terms_recv,
    tile, tile_send, tile_recv,
    sums, sums_send, sums_recv, pair, pair_send, pair_recv,
    hot_first, hot_middle, hot_last, flat_rhs, flat_self, flat_along, pick,
):
    r = lax.axis_index("rows")
    b = lax.axis_index("bal")
    z, c = r // 2, r % 2
    x, y = b // 4, b % 4

    def along_z(i, core=c):
        return (((z + i + 16) % 16) * 2 + core, b)

    def in_plane(j):
        jx, jy = j // 4, j % 4
        px = x + jx - 2 * (x % 2) * (jx % 2) - 4 * ((x // 2) * (jx // 2))
        py = y + jy - 2 * (y % 2) * (jy % 2) - 4 * ((y // 2) * (jy // 2))
        return px * 4 + py

    sibling = (z * 2 + 1 - c, b)
    peer = {j: in_plane(j) for j in PLANE}
    both = [i for i in ALONG if RANKS[i] > 8]

    barrier = pltpu.get_barrier_semaphore()
    for i in ALONG:
        pl.semaphore_signal(barrier, inc=1, device_id=along_z(i), device_id_type=MESH)
    for i in both:
        pl.semaphore_signal(barrier, inc=1, device_id=along_z(i, 1 - c), device_id_type=MESH)
    for j in PLANE:
        pl.semaphore_signal(barrier, inc=1, device_id=(r, peer[j]), device_id_type=MESH)
    pl.semaphore_signal(barrier, inc=1, device_id=sibling, device_id_type=MESH)

    loads = [
        pltpu.make_async_copy(a, v, load_sem.at[n])
        for n, (a, v) in enumerate(
            (
                (rhs_hbm, rhs), (self_hbm, self_term), (near_row_hbm, near_row), (far_row_hbm, far_row),
                (near_col_hbm, near_col), (far_col_hbm, far_col), (far_rank_hbm, far_rank),
                (near_hbm, near), (left_hbm, left), (right_hbm, right),
            )
        )
    ]
    for load in loads:
        load.start()
    for load in loads[:7]:
        load.wait()

    def halves(value):
        return jnp.concatenate([value[:, :128], value[:, 128:]], axis=0)

    own_rhs = halves(rhs[...])
    own[...] = own_rhs
    along[0] = own_rhs

    base = r * 32
    lane = lax.broadcasted_iota(jnp.int32, (4, 128), 0) * 128 + lax.broadcasted_iota(jnp.int32, (4, 128), 1)
    mine = ((lane >> 4) & 15) == b
    half_of = (lane >> 3) & 1
    task_of = (lane & 7) + 8 * (lane >> 8)
    row_of = jnp.full((4, 128), -1, jnp.int32)
    for k in range(NEAR + FARS):
        local = (near_row[k] if k < NEAR else far_row[k - NEAR]) - base
        row_of = jnp.where(mine & (task_of == k), 2 * local - (local & 1), row_of)
    place = jnp.where(row_of >= 0, row_of + 2 * half_of + 1, 0).astype(F32)
    plane[b] = jnp.concatenate([own_rhs, halves(self_term[...]), place, jnp.zeros((4, 128), F32)], axis=0)

    pl.semaphore_wait(barrier, 31 + len(both))

    pending = []

    def send(src, dst, send_sem, recv_sem, device):
        pltpu.make_async_remote_copy(
            src_ref=src, dst_ref=dst, send_sem=send_sem, recv_sem=recv_sem, device_id=device, device_id_type=MESH
        ).start()

    def whole_stage(ref, send_sem, recv_sem):
        return pltpu.make_async_remote_copy(
            src_ref=ref, dst_ref=ref, send_sem=send_sem, recv_sem=recv_sem, device_id=sibling, device_id_type=MESH
        )

    def arrived(ref, recv_sem):
        whole_stage(ref, recv_sem, recv_sem).wait_recv()

    def sending(ref, send_sem):
        pending.append(whole_stage(ref, send_sem, send_sem))

    def settle():
        while pending:
            pending.pop().wait_send()

    for i in ALONG:
        rank = RANKS[i]
        batch = (rank // 4 + 1) // 2
        send(own, along.at[rank], along_send.at[0], along_recv.at[batch], along_z(i))
        if batch == 2:
            send(own, along.at[rank + 4], along_send.at[0], along_recv.at[batch], along_z(i, 1 - c))
    sending(along.at[0:19], along_send.at[0])
    for j in PLANE:
        send(plane.at[b], plane.at[b], plane_send.at[0], plane_recv.at[0], (r, peer[j]))
    sending(plane.at[0:15], plane_send.at[0])

    task = lax.broadcasted_iota(jnp.int32, (32, 1), 0)
    half = task >> 4
    place_1 = jnp.full((32, 1), -1, jnp.int32)
    place_2 = jnp.full((32, 1), -1, jnp.int32)
    for k in range(NEAR + FARS):
        col = near_col[k] if k < NEAR else far_col[k - NEAR]
        other = ((col >> 5) & 1) ^ c
        d = ((col >> 6) - z + 16) & 15
        dev = (col >> 1) & 15
        cl = col & 1
        rank = jnp.where(d == 0, 0, jnp.where(d <= 8, 2 * d - 1, 32 - 2 * d))
        tile_of, low = rank >> 2, rank & 3

        def spot_of(holder, row):
            in_first = other * 256 + holder * 16 + row
            in_middle = 512 + other * 512 + holder * 32 + (tile_of - 1) * 16 + row
            in_last = 1536 + holder * 32 + other * 16 + row
            return jnp.where(tile_of == 0, in_first, jnp.where(tile_of == 3, in_last, in_middle))

        p1 = spot_of(dev, low * 4 + cl)
        p2 = spot_of(low * 4 + (dev >> 2), (dev & 3) * 4 + cl)
        place_1 = jnp.where((task & 15) == k, p1 + 2 * half, place_1)
        place_2 = jnp.where((task & 15) == k, p2 + 2 * half, place_2)
    spot = lax.broadcasted_iota(jnp.int32, (32, 512), 1)

    def hots(place, start, size):
        return jnp.where(spot[:, :size] + start == place, 1.0, 0.0).astype(BF16)

    for it, place in ((0, place_1), (1, place_2)):
        for other in range(2):
            hot_first[it, other] = hots(place, 256 * other, 256)
            hot_middle[it, other] = hots(place, 512 + 512 * other, 512)
        hot_last[it] = hots(place, 1536, 512)

    rank_of = jnp.zeros((16, 1), jnp.int32)
    task16 = lax.broadcasted_iota(jnp.int32, (16, 1), 0)
    for k in range(FARS):
        rank_of = jnp.where(task16 == NEAR + k, far_rank[k], rank_of)
    lane192 = lax.broadcasted_iota(jnp.int32, (16, FARS * RANK), 1)
    keep = ((lane192 >> 5) + NEAR == task16) & ((lane192 & 31) < rank_of)

    own_tiles = [[first_tiles.at[it, 0], middle_tiles.at[it, 0], last_tiles.at[it]] for it in range(2)]

    def send_batch(it, batch):
        held = own_tiles[it][batch]
        for j in PLANE:
            part = held.at[b]
            send(part, part, gather_send.at[it, batch], gather_recv.at[it, batch], (r, peer[j]))
        sending(held.at[0:15], gather_send.at[it, batch])

    def finish_batch(it, batch):
        held = own_tiles[it][batch]
        arrived(held.at[0:15], gather_recv.at[it, batch])
        if batch < 2:
            there = (first_tiles, middle_tiles)[batch].at[it, 1]
            send(held, there, core_send.at[it, batch], core_recv.at[it, batch], sibling)
            sending(held, core_send.at[it, batch])

    def picked(hot, source):
        return jnp.dot(hot, source.reshape(-1, 128), preferred_element_type=F32)

    def joined(value):
        return jnp.concatenate([value[:16], value[16:]], axis=1)

    def send_terms(it, kind, value):
        terms[it, kind, b] = halves(value).astype(BF16)
        for j in PLANE:
            part = terms.at[it, kind, b]
            send(part, part, terms_send.at[it, kind], terms_recv.at[it, kind], (r, peer[j]))
        sending(terms.at[it, kind, 0:15], terms_send.at[it, kind])

    def take_terms(it, kind, select):
        arrived(terms.at[it, kind, 0:15], terms_recv.at[it, kind])
        return jnp.dot(select, terms[it, kind].reshape(256, 128), preferred_element_type=F32)

    def near_terms(picks):
        source = joined(picks)
        result = jnp.zeros((16, 256), F32)
        for k in range(NEAR):
            one = jnp.where(task16 == k, source, 0.0).astype(BF16)
            result += lax.dot_general(one, near[k], (((1,), (1,)), ((), ())), preferred_element_type=F32)
        return result[:8]

    def far_terms(picks):
        source = joined(picks).astype(BF16)
        coeff = lax.dot_general(
            source, right[...].reshape(FARS * RANK, 256), (((1,), (1,)), ((), ())), preferred_element_type=F32
        )
        coeff = jnp.where(keep, coeff, 0.0).astype(BF16)
        return jnp.dot(coeff, left[...].reshape(FARS * RANK, 256), preferred_element_type=F32)[8:]

    def send_sums(stage, values):
        lanes = lax.broadcasted_iota(jnp.int32, (1, 128), 1)
        row = jnp.zeros((1, 128), F32)
        for n, value in enumerate(values):
            row = jnp.where(lanes == n, value, row)
        sums[stage, 0] = row
        for i in ALONG:
            slot = RANKS[i]
            far = int(slot > 8)
            send(sums.at[stage, 0], sums.at[stage, slot], sums_send.at[stage], sums_recv.at[stage, far], along_z(i))
            if far and stage == 2:
                there = sums.at[stage, slot + 7]
                send(sums.at[stage, 0], there, sums_send.at[stage], sums_recv.at[stage, 1], along_z(i, 1 - c))
        sending(sums.at[stage, 0 : 22 if stage == 2 else 15], sums_send.at[stage])

    def pair_sums(stage):
        arrived(sums.at[stage, 0:8], sums_recv.at[stage, 0])
        if stage < 2:
            arrived(sums.at[stage, 0:7], sums_recv.at[stage, 1])
        pair[stage, 0] = jnp.sum(sums[stage, 0 : 9 if stage == 2 else 16], axis=0)
        send(pair.at[stage, 0], pair.at[stage, 1], pair_send.at[stage], pair_recv.at[stage], sibling)
        sending(pair.at[stage, 0], pair_send.at[stage])

    def take_sums(stage, count):
        arrived(pair.at[stage, 1], pair_recv.at[stage])
        row = pair[stage, 0] + pair[stage, 1]
        if stage == 2:
            arrived(sums.at[stage, 0:14], sums_recv.at[stage, 1])
            row += jnp.sum(sums[stage, 9:23], axis=0)
        return [row[:, n : n + 1] for n in range(count)]

    for batch, (start, stop, count) in enumerate(BOUNDS):
        arrived(along.at[0:count], along_recv.at[batch])
        for e in range(start, stop):
            flat_along[4 * e : 4 * e + 4] = along[e]
        part = flat_along[4 * start : 4 * stop].astype(BF16)
        own_tiles[0][batch][b] = part if batch == 0 else part.reshape(2, 16, 128)
        send_batch(0, batch)

    arrived(plane.at[0:15], plane_recv.at[0])
    index = jnp.zeros((4, 128), F32)
    for dev in range(16):
        flat_rhs[4 * dev : 4 * dev + 4] = plane[dev, 0:4]
        flat_self[4 * dev : 4 * dev + 4] = plane[dev, 4:8]
        index += plane[dev, 8:12]
    squares = flat_rhs[...] * flat_rhs[...]
    send_sums(0, [total(squares), total(squares * flat_self[...])])
    index = index.astype(jnp.int32)
    spots = lax.broadcasted_iota(jnp.int32, (64, 256), 0) + 1
    selects = [
        jnp.where(
            spots == jnp.concatenate([index[2 * kind : 2 * kind + 1], index[2 * kind + 1 : 2 * kind + 2]], axis=1),
            1.0, 0.0,
        ).astype(BF16)
        for kind in range(2)
    ]

    def operate(it):
        finish_batch(it, 0)
        picks = picked(hot_first[it, 0], first_tiles[it, 0])
        arrived(first_tiles.at[it, 1], core_recv.at[it, 0])
        picks += picked(hot_first[it, 1], first_tiles[it, 1])
        if it == 0:
            for load in loads[7:]:
                load.wait()
        send_terms(it, 0, near_terms(picks))
        pick[...] = picks
        finish_batch(it, 1)
        picks = pick[...] + picked(hot_middle[it, 0], middle_tiles[it, 0])
        arrived(middle_tiles.at[it, 1], core_recv.at[it, 1])
        picks += picked(hot_middle[it, 1], middle_tiles[it, 1])
        finish_batch(it, 2)
        picks += picked(hot_last[it], last_tiles[it])
        send_terms(it, 1, far_terms(picks))
        pair_sums(it)
        image = take_terms(it, 0, selects[0])
        return image + take_terms(it, 1, selects[1])

    image = operate(0)
    beta_squared, diagonal = take_sums(0, 2)
    beta = jnp.sqrt(beta_squared)
    guess = diagonal / beta_squared
    inverse = 1.0 / beta
    first = flat_rhs[...] * inverse
    image = (flat_self[...] * flat_rhs[...] + image) * inverse
    shifted = image - guess * first

    tile[...] = shifted.astype(BF16).reshape(4, 16, 128)

    def tile_copy(n, core=0):
        rank = 4 * n + x
        away = (rank + 1) // 2
        d = away * (2 * (rank % 2) - 1)
        held = own_tiles[1][(n + 1) // 2].at[b]
        part = held if n == 0 else held.at[n - 1] if n < 3 else held.at[core]
        return pltpu.make_async_remote_copy(
            src_ref=tile.at[y], dst_ref=part, send_sem=tile_send.at[n + core], recv_sem=tile_recv.at[n + core],
            device_id=along_z(-d, 1 - c if core else c), device_id_type=MESH,
        )

    far_tiles = [tile_copy(3), tile_copy(3, 1), tile_copy(2), tile_copy(1)]
    for copy in far_tiles:
        copy.start()

    @pl.when(x > 0)
    def _():
        tile_copy(0).start()

    @pl.when(x == 0)
    def _():
        first_tiles[1, 0, b] = tile[y]

    send_sums(1, [total(first * first), total(first * shifted), total(shifted * shifted)])

    @pl.when(x > 0)
    def _():
        tile_copy(0).wait_recv()

    send_batch(1, 0)
    far_tiles[3].wait_recv()
    far_tiles[2].wait_recv()
    send_batch(1, 1)
    far_tiles[0].wait_recv()
    far_tiles[1].wait_recv()
    send_batch(1, 2)

    second = operate(1)
    g11, p1, p2 = take_sums(1, 3)
    h11 = guess * g11 + p1
    step = h11 - guess
    h21 = jnp.sqrt(jnp.maximum(p2 - 2.0 * step * p1 + step * step * g11, 0.0) + 1e-06)
    inverse = 1.0 / h21
    second = (flat_self[...] * shifted + second - step * image) * inverse
    basis = (shifted - step * first) * inverse
    rest = second - guess * basis
    send_sums(
        2,
        [total(first * rest), total(basis * rest), total(rest * rest), total(first * basis), total(basis * basis)],
    )

    def mine_of(value):
        flat_along[0:64] = value
        two = flat_along[pl.ds(pl.multiple_of((b // 2) * 8, 8), 8), :]
        return jnp.where(b % 2 == 0, two[:4], two[4:])

    own_first, own_basis, own_rest = mine_of(first), mine_of(basis), mine_of(rest)
    for copy in far_tiles:
        copy.wait_send()

    @pl.when(x > 0)
    def _():
        tile_copy(0).wait_send()

    settle()

    pair_sums(2)
    q1, q2, q3, g12, g22 = take_sums(2, 5)
    h12 = q1 + guess * g12
    h22 = q2 + guess * g22
    left_over = h22 - guess
    square = (
        q3 - 2.0 * h12 * q1 - 2.0 * left_over * q2
        + h12 * h12 * g11 + left_over * left_over * g22 + 2.0 * h12 * left_over * g12
    )
    h32 = jnp.sqrt(jnp.maximum(square, 0.0) + 1e-06)

    radius = jnp.sqrt(h11 * h11 + h21 * h21)
    cosine = h11 / radius
    sine = h21 / radius
    upper = cosine * h12 + sine * h22
    lower = cosine * h22 - sine * h12
    radius_two = jnp.sqrt(lower * lower + h32 * h32)
    coef_two = -(lower / radius_two) * sine * beta / radius_two
    coef_one = (cosine * beta - upper * coef_two) / radius

    def wide(value):
        return jnp.concatenate([value[0:2], value[2:4]], axis=1)

    out[0] = wide(coef_one * own_first + coef_two * own_basis)
    out[1] = wide((own_rest - h12 * own_first - left_over * own_basis) / h32)

    settle()


def shards(rhs, self_term, near_blocks, near_row, near_col, far_left, far_right, far_row, far_col, far_rank):
    hbm = pl.BlockSpec(memory_space=pltpu.HBM)
    dma = pltpu.SemaphoreType.DMA
    out = pl.pallas_call(
        kernel,
        out_shape=jax.ShapeDtypeStruct((2, *rhs.shape), F32),
        in_specs=[hbm] * 10,
        out_specs=pl.BlockSpec(memory_space=pltpu.VMEM),
        scratch_shapes=[
            *[pltpu.SMEM(a.shape, jnp.int32) for a in (near_row, near_col, far_row, far_col, far_rank)],
            pltpu.VMEM(rhs.shape, F32), pltpu.VMEM(rhs.shape, F32),
            pltpu.VMEM(near_blocks.shape, BF16), pltpu.VMEM(far_left.shape, BF16), pltpu.VMEM(far_right.shape, BF16),
            dma((10,)),
            pltpu.VMEM((4, 128), F32), pltpu.VMEM((20, 4, 128), F32), dma((1,)), dma((3,)),
            pltpu.VMEM((16, 16, 128), F32), dma((1,)), dma((1,)),
            pltpu.VMEM((2, 2, 16, 16, 128), BF16), pltpu.VMEM((2, 2, 16, 2, 16, 128), BF16),
            pltpu.VMEM((2, 16, 2, 16, 128), BF16), dma((2, 3)), dma((2, 3)), dma((2, 2)), dma((2, 2)),
            pltpu.VMEM((2, 2, 16, 16, 128), BF16), dma((2, 2)), dma((2, 2)),
            pltpu.VMEM((4, 16, 128), BF16), dma((5,)), dma((5,)),
            pltpu.VMEM((3, 23, 1, 128), F32), dma((3,)), dma((3, 2)),
            pltpu.VMEM((3, 2, 1, 128), F32), dma((3,)), dma((3,)),
            pltpu.VMEM((2, 2, 32, 256), BF16), pltpu.VMEM((2, 2, 32, 512), BF16), pltpu.VMEM((2, 32, 512), BF16),
            pltpu.VMEM((64, 128), F32), pltpu.VMEM((64, 128), F32), pltpu.VMEM((80, 128), F32),
            pltpu.VMEM((32, 128), F32),
        ],
        compiler_params=pltpu.CompilerParams(
            collective_id=0, has_side_effects=True, vmem_limit_bytes=56 * 1024 * 1024
        ),
        name="gmres",
    )(near_row, near_col, far_row, far_col, far_rank, rhs, self_term, near_blocks, far_left, far_right)
    return out[0], out[1]


def solution(mesh):
    vec = P(("rows", "bal"), None)
    blocks = P(("rows", "bal"), None, None)
    ints = P(("rows", "bal"))
    in_specs = (vec, vec, blocks, ints, ints, blocks, blocks, ints, ints, ints)
    return jax.shard_map(shards, mesh=mesh, in_specs=in_specs, out_specs=(vec, vec), check_vma=False)
```

time: 76.2 us -> 61.8 us (0.81)
  local copies, waits for them, and re-layouts: 8.8 us -> 1.26 us
  Pallas kernels: 66.4 us -> 59.7 us
    unnamed x22 -> x0, local copies, waits for them, and re-layouts: 8.8 us -> none
    pallas_call x1, Pallas kernels: 66.4 us -> 59.7 us  [shards(): pl.pallas_call(kernel, out_shape=jax.ShapeDtypeStruct((2, *rhs.shape), F3...]
    squeeze x0 -> x1, local copies, waits for them, and re-layouts: none -> 1.26 us  [shards(): return (out[0], out[1])]
where the time goes in v2:
time: 61.8 us; the launch traced here: 61.6 us
  Pallas kernels  59.7 us (97%)
  local copies, waits for them, and re-layouts  1.26 us (2%)
  between operations  0.64 us (1%)
    pallas_call x1, Pallas kernels, shards(): pl.pallas_call(kernel, out_shape=jax.ShapeDtypeStruct((2, *rhs.shape), F3...  59.7 us
    squeeze x1, local copies, waits for them, and re-layouts, shards(): return (out[0], out[1])  1.26 us

profile of v2, /device:TPU:1, one launch (start us, length us, event | category | flops | bytes accessed | tf_op | source)
XLA Modules:
  0.0 61.6 jit_solution(3934397830737841900)
XLA Ops:
  0.6 59.7 %gmres.1 = f32[2,2,256]{2,1,0:T(2,128)} custom-call(s32[8]{0:T(128)} %near_row_hbm.1, s32[8]{0:T(128)} %near_col_hbm.1, s32[6]{0:T(128)} %far_row_hbm.1, s32[6]{0:T(128)} %far_col_hbm.1, s32[6]{0:T(128)} %far_rank_hbm.1, f32[2,256]{1,0:T(2,128)} %rhs_hbm.1, f32[2,256]{1,0:T(2,128)} %self_hbm.1, bf16[8,256,256]{2,1,0:T(8,128)(2,1)} %near_hbm.1, ...), custom_call_target="tpu_custom_call" | custom-call | tf_op jit(solution)/shard_map/gmres/pallas_call | solution.py:422
  60.4 1.3 %slice_bitcast_fusion = (f32[2,256]{1,0:T(2,128)}, f32[2,256]{1,0:T(2,128)}) fusion(f32[2,2,256]{2,1,0:T(2,128)} %gmres.1), kind=kLoop, calls=%fused_computation | loop fusion | bytes 8192 | tf_op jit(solution)/shard_map/squeeze | solution.py:449

commit v3 on v2

--- a/solution.py
+++ b/solution.py
@@ -24,6 +24,7 @@
 
 
 RANKS = {i: ranked(signed(-i % 16)) for i in ALONG}
+OFFSETS = ((0, 0), (0, 1), (2, 0), (0, 3), (1, 0), (1, 1), (3, 0), (3, 1))
 BOUNDS = ((0, 4, 3), (4, 12, 8), (12, 20, 8))
 
 
@@ -39,7 +40,7 @@
     near, left, right, load_sem,
     own, along, along_send, along_recv,
     plane, plane_send, plane_recv,
-    first_tiles, middle_tiles, last_tiles, gather_send, gather_recv, core_send, core_recv,
+    first_1, middle_1, last_1, first_2, middle_2, last_2, gather_send, gather_recv, core_send, core_recv,
     terms, terms_send, terms_recv,
     tile, tile_send, tile_recv,
     sums, sums_send, sums_recv, pair, pair_send, pair_recv,
@@ -154,14 +155,19 @@
         rank = jnp.where(d == 0, 0, jnp.where(d <= 8, 2 * d - 1, 32 - 2 * d))
         tile_of, low = rank >> 2, rank & 3
 
-        def spot_of(holder, row):
-            in_first = other * 256 + holder * 16 + row
-            in_middle = 512 + other * 512 + holder * 32 + (tile_of - 1) * 16 + row
-            in_last = 1536 + holder * 32 + other * 16 + row
-            return jnp.where(tile_of == 0, in_first, jnp.where(tile_of == 3, in_last, in_middle))
-
-        p1 = spot_of(dev, low * 4 + cl)
-        p2 = spot_of(low * 4 + (dev >> 2), (dev & 3) * 4 + cl)
+        row = low * 4 + cl
+        in_first = other * 256 + dev * 16 + row
+        in_middle = 512 + other * 512 + dev * 32 + (tile_of - 1) * 16 + row
+        in_last = 1536 + dev * 32 + other * 16 + row
+        p1 = jnp.where(tile_of == 0, in_first, jnp.where(tile_of == 3, in_last, in_middle))
+        t = rank >> 1
+        away = ((rank ^ t) & 1) ^ (x % 2)
+        slot = away * 4 + (((dev >> 2) - y - 2 * (((x + away) & 3) >> 1) + 8) & 3)
+        row = (dev & 3) * 4 + cl
+        in_first = ((other * 8 + slot) * 2 + t) * 16 + row
+        in_middle = 512 + ((other * 8 + slot) * 4 + t - 2) * 16 + row
+        in_last = 1536 + ((slot * 2 + other) * 2 + t - 6) * 16 + row
+        p2 = jnp.where(t < 2, in_first, jnp.where(t >= 6, in_last, in_middle))
         place_1 = jnp.where((task & 15) == k, p1 + 2 * half, place_1)
         place_2 = jnp.where((task & 15) == k, p2 + 2 * half, place_2)
     spot = lax.broadcasted_iota(jnp.int32, (32, 512), 1)
@@ -182,21 +188,27 @@
     lane192 = lax.broadcasted_iota(jnp.int32, (16, FARS * RANK), 1)
     keep = ((lane192 >> 5) + NEAR == task16) & ((lane192 & 31) < rank_of)
 
-    own_tiles = [[first_tiles.at[it, 0], middle_tiles.at[it, 0], last_tiles.at[it]] for it in range(2)]
+    own_tiles = [[first_1.at[0], middle_1.at[0], last_1], [first_2.at[0], middle_2.at[0], last_2]]
+    other_tiles = [[first_1.at[1], middle_1.at[1]], [first_2.at[1], middle_2.at[1]]]
 
     def send_batch(it, batch):
         held = own_tiles[it][batch]
-        for j in PLANE:
-            part = held.at[b]
-            send(part, part, gather_send.at[it, batch], gather_recv.at[it, batch], (r, peer[j]))
-        sending(held.at[0:15], gather_send.at[it, batch])
+        if it == 0:
+            for j in PLANE:
+                send(held.at[b], held.at[b], gather_send.at[it, batch], gather_recv.at[it, batch], (r, peer[j]))
+            sending(held.at[0:15], gather_send.at[it, batch])
+        else:
+            for slot in (2, 5, 7, 1, 3, 4, 6):
+                ox, oy = OFFSETS[slot]
+                to = (r, ((x - ox + 4) % 4) * 4 + (y - oy + 4) % 4)
+                send(held.at[0], held.at[slot], gather_send.at[it, batch], gather_recv.at[it, batch], to)
+            sending(held.at[0:7], gather_send.at[it, batch])
 
     def finish_batch(it, batch):
         held = own_tiles[it][batch]
-        arrived(held.at[0:15], gather_recv.at[it, batch])
+        arrived(held.at[0 : 7 if it else 15], gather_recv.at[it, batch])
         if batch < 2:
-            there = (first_tiles, middle_tiles)[batch].at[it, 1]
-            send(held, there, core_send.at[it, batch], core_recv.at[it, batch], sibling)
+            send(held, other_tiles[it][batch], core_send.at[it, batch], core_recv.at[it, batch], sibling)
             sending(held, core_send.at[it, batch])
 
     def picked(hot, source):
@@ -289,88 +301,99 @@
         for kind in range(2)
     ]
 
-    def operate(it):
+    def operate(it, before):
         finish_batch(it, 0)
-        picks = picked(hot_first[it, 0], first_tiles[it, 0])
-        arrived(first_tiles.at[it, 1], core_recv.at[it, 0])
-        picks += picked(hot_first[it, 1], first_tiles[it, 1])
+        picks = picked(hot_first[it, 0], own_tiles[it][0][...])
+        arrived(other_tiles[it][0], core_recv.at[it, 0])
+        picks += picked(hot_first[it, 1], other_tiles[it][0][...])
         if it == 0:
             for load in loads[7:]:
                 load.wait()
         send_terms(it, 0, near_terms(picks))
         pick[...] = picks
         finish_batch(it, 1)
-        picks = pick[...] + picked(hot_middle[it, 0], middle_tiles[it, 0])
-        arrived(middle_tiles.at[it, 1], core_recv.at[it, 1])
-        picks += picked(hot_middle[it, 1], middle_tiles[it, 1])
+        picks = pick[...] + picked(hot_middle[it, 0], own_tiles[it][1][...])
+        arrived(other_tiles[it][1], core_recv.at[it, 1])
+        picks += picked(hot_middle[it, 1], other_tiles[it][1][...])
         finish_batch(it, 2)
-        picks += picked(hot_last[it], last_tiles[it])
+        picks += picked(hot_last[it], own_tiles[it][2][...])
         send_terms(it, 1, far_terms(picks))
         pair_sums(it)
-        image = take_terms(it, 0, selects[0])
-        return image + take_terms(it, 1, selects[1])
-
-    image = operate(0)
-    beta_squared, diagonal = take_sums(0, 2)
-    beta = jnp.sqrt(beta_squared)
-    guess = diagonal / beta_squared
-    inverse = 1.0 / beta
-    first = flat_rhs[...] * inverse
-    image = (flat_self[...] * flat_rhs[...] + image) * inverse
-    shifted = image - guess * first
+        known = before(take_terms(it, 0, selects[0]))
+        return known, take_terms(it, 1, selects[1])
+
+    def before_1(sums_near):
+        beta_squared, diagonal = take_sums(0, 2)
+        beta = jnp.sqrt(beta_squared)
+        guess = diagonal / beta_squared
+        inverse = 1.0 / beta
+        first = flat_rhs[...] * inverse
+        image = (flat_self[...] * flat_rhs[...] + sums_near) * inverse
+        return beta, guess, inverse, first, image, image - guess * first, total(first * first)
+
+    (beta, guess, inverse, first, image, shifted, g11_here), sums_far = operate(0, before_1)
+    sums_far = sums_far * inverse
+    image = image + sums_far
+    shifted = shifted + sums_far
 
     tile[...] = shifted.astype(BF16).reshape(4, 16, 128)
 
-    def tile_copy(n, core=0):
-        rank = 4 * n + x
+    even, quarter = x % 2, (y + 2 * (x // 2)) % 4
+
+    def tile_copy(t, core=0):
+        rank = 2 * t + (1 - even if t % 2 else even)
         away = (rank + 1) // 2
         d = away * (2 * (rank % 2) - 1)
-        held = own_tiles[1][(n + 1) // 2].at[b]
-        part = held if n == 0 else held.at[n - 1] if n < 3 else held.at[core]
+        batch = (t + 2) // 4
+        held = own_tiles[1][batch].at[0]
+        part = held.at[t] if batch == 0 else held.at[t - 2] if batch == 1 else held.at[core, t - 6]
+        recv = tile_recv.at[t if batch == 0 else batch + 1]
         return pltpu.make_async_remote_copy(
-            src_ref=tile.at[y], dst_ref=part, send_sem=tile_send.at[n + core], recv_sem=tile_recv.at[n + core],
+            src_ref=tile.at[quarter], dst_ref=part, send_sem=tile_send.at[int(t > 0)], recv_sem=recv,
             device_id=along_z(-d, 1 - c if core else c), device_id_type=MESH,
         )
 
-    far_tiles = [tile_copy(3), tile_copy(3, 1), tile_copy(2), tile_copy(1)]
-    for copy in far_tiles:
-        copy.start()
-
-    @pl.when(x > 0)
+    for t, core in ((7, 0), (7, 1), (6, 0), (6, 1), (5, 0), (4, 0), (3, 0), (2, 0), (1, 0)):
+        tile_copy(t, core).start()
+    sending(first_2.at[0, 0:4, 0], tile_send.at[1])
+    sending(middle_2.at[0, 0, 0:4], tile_send.at[1])
+    sending(first_2.at[0, 0, 0:1], tile_send.at[1])
+
+    @pl.when(even > 0)
     def _():
         tile_copy(0).start()
 
-    @pl.when(x == 0)
+    @pl.when(even == 0)
     def _():
-        first_tiles[1, 0, b] = tile[y]
-
-    send_sums(1, [total(first * first), total(first * shifted), total(shifted * shifted)])
-
-    @pl.when(x > 0)
+        first_2[0, 0, 0] = tile[quarter]
+
+    send_sums(1, [g11_here, total(first * shifted), total(shifted * shifted)])
+
+    @pl.when(even > 0)
     def _():
         tile_copy(0).wait_recv()
 
+    tile_copy(1).wait_recv()
     send_batch(1, 0)
-    far_tiles[3].wait_recv()
-    far_tiles[2].wait_recv()
+    arrived(middle_2.at[0, 0], tile_recv.at[2])
     send_batch(1, 1)
-    far_tiles[0].wait_recv()
-    far_tiles[1].wait_recv()
+    arrived(last_2.at[0], tile_recv.at[3])
     send_batch(1, 2)
 
-    second = operate(1)
-    g11, p1, p2 = take_sums(1, 3)
-    h11 = guess * g11 + p1
-    step = h11 - guess
-    h21 = jnp.sqrt(jnp.maximum(p2 - 2.0 * step * p1 + step * step * g11, 0.0) + 1e-06)
-    inverse = 1.0 / h21
-    second = (flat_self[...] * shifted + second - step * image) * inverse
-    basis = (shifted - step * first) * inverse
-    rest = second - guess * basis
-    send_sums(
-        2,
-        [total(first * rest), total(basis * rest), total(rest * rest), total(first * basis), total(basis * basis)],
-    )
+    def before_2(sums_near):
+        g11, p1, p2 = take_sums(1, 3)
+        h11 = guess * g11 + p1
+        step = h11 - guess
+        h21 = jnp.sqrt(jnp.maximum(p2 - 2.0 * step * p1 + step * step * g11, 0.0) + 1e-06)
+        inverse = 1.0 / h21
+        basis = (shifted - step * first) * inverse
+        rest = (flat_self[...] * shifted + sums_near - step * image) * inverse - guess * basis
+        radius = jnp.sqrt(h11 * h11 + h21 * h21)
+        return g11, h11, h21, inverse, basis, rest, radius, total(first * basis), total(basis * basis)
+
+    (g11, h11, h21, inverse, basis, rest, radius, g12_here, g22_here), sums_far = operate(1, before_2)
+    rest = rest + sums_far * inverse
+    send_sums(2, [total(first * rest), total(basis * rest), total(rest * rest), g12_here, g22_here])
 
     def mine_of(value):
         flat_along[0:64] = value
@@ -378,10 +401,11 @@
         return jnp.where(b % 2 == 0, two[:4], two[4:])
 
     own_first, own_basis, own_rest = mine_of(first), mine_of(basis), mine_of(rest)
-    for copy in far_tiles:
-        copy.wait_send()
-
-    @pl.when(x > 0)
+    turn = 1.0 / radius
+    cosine = h11 * turn
+    sine = h21 * turn
+
+    @pl.when(even > 0)
     def _():
         tile_copy(0).wait_send()
 
@@ -396,22 +420,17 @@
         q3 - 2.0 * h12 * q1 - 2.0 * left_over * q2
         + h12 * h12 * g11 + left_over * left_over * g22 + 2.0 * h12 * left_over * g12
     )
-    h32 = jnp.sqrt(jnp.maximum(square, 0.0) + 1e-06)
-
-    radius = jnp.sqrt(h11 * h11 + h21 * h21)
-    cosine = h11 / radius
-    sine = h21 / radius
+    square = jnp.maximum(square, 0.0) + 1e-06
     upper = cosine * h12 + sine * h22
     lower = cosine * h22 - sine * h12
-    radius_two = jnp.sqrt(lower * lower + h32 * h32)
-    coef_two = -(lower / radius_two) * sine * beta / radius_two
-    coef_one = (cosine * beta - upper * coef_two) / radius
+    coef_two = -(lower / (lower * lower + square)) * (sine * beta)
+    coef_one = (cosine * beta - upper * coef_two) * turn
 
     def wide(value):
         return jnp.concatenate([value[0:2], value[2:4]], axis=1)
 
     out[0] = wide(coef_one * own_first + coef_two * own_basis)
-    out[1] = wide((own_rest - h12 * own_first - left_over * own_basis) / h32)
+    out[1] = wide((own_rest - h12 * own_first - left_over * own_basis) * lax.rsqrt(square))
 
     settle()
 
@@ -431,10 +450,11 @@
             dma((10,)),
             pltpu.VMEM((4, 128), F32), pltpu.VMEM((20, 4, 128), F32), dma((1,)), dma((3,)),
             pltpu.VMEM((16, 16, 128), F32), dma((1,)), dma((1,)),
-            pltpu.VMEM((2, 2, 16, 16, 128), BF16), pltpu.VMEM((2, 2, 16, 2, 16, 128), BF16),
-            pltpu.VMEM((2, 16, 2, 16, 128), BF16), dma((2, 3)), dma((2, 3)), dma((2, 2)), dma((2, 2)),
+            pltpu.VMEM((2, 16, 16, 128), BF16), pltpu.VMEM((2, 16, 2, 16, 128), BF16), pltpu.VMEM((16, 2, 16, 128), BF16),
+            pltpu.VMEM((2, 8, 2, 16, 128), BF16), pltpu.VMEM((2, 8, 4, 16, 128), BF16),
+            pltpu.VMEM((8, 2, 2, 16, 128), BF16), dma((2, 3)), dma((2, 3)), dma((2, 2)), dma((2, 2)),
             pltpu.VMEM((2, 2, 16, 16, 128), BF16), dma((2, 2)), dma((2, 2)),
-            pltpu.VMEM((4, 16, 128), BF16), dma((5,)), dma((5,)),
+            pltpu.VMEM((4, 16, 128), BF16), dma((2,)), dma((4,)),
             pltpu.VMEM((3, 23, 1, 128), F32), dma((3,)), dma((3, 2)),
             pltpu.VMEM((3, 2, 1, 128), F32), dma((3,)), dma((3,)),
             pltpu.VMEM((2, 2, 32, 256), BF16), pltpu.VMEM((2, 2, 32, 512), BF16), pltpu.VMEM((2, 32, 512), BF16),

time: 61.8 us -> 61.3 us (level)
  no operation moved by 1% of the time
where the time goes in v3:
time: 61.3 us; the launch traced here: 61.1 us
  Pallas kernels  59.2 us (97%)
  local copies, waits for them, and re-layouts  1.26 us (2%)
  between operations  0.64 us (1%)
    pallas_call x1, Pallas kernels, shards(): pl.pallas_call(kernel, out_shape=jax.ShapeDtypeStruct((2, *rhs.shape), F3...  59.2 us
    squeeze x1, local copies, waits for them, and re-layouts, shards(): return (out[0], out[1])  1.26 us

profile of v3, /device:TPU:1, one launch (start us, length us, event | category | flops | bytes accessed | tf_op | source)
XLA Modules:
  0.0 61.1 jit_solution(18094159373258881346)
XLA Ops:
  0.6 59.2 %gmres.1 = f32[2,2,256]{2,1,0:T(2,128)} custom-call(s32[8]{0:T(128)} %near_row_hbm.1, s32[8]{0:T(128)} %near_col_hbm.1, s32[6]{0:T(128)} %far_row_hbm.1, s32[6]{0:T(128)} %far_col_hbm.1, s32[6]{0:T(128)} %far_rank_hbm.1, f32[2,256]{1,0:T(2,128)} %rhs_hbm.1, f32[2,256]{1,0:T(2,128)} %self_hbm.1, bf16[8,256,256]{2,1,0:T(8,128)(2,1)} %near_hbm.1, ...), custom_call_target="tpu_custom_call" | custom-call | tf_op jit(solution)/shard_map/gmres/pallas_call | solution.py:441
  59.9 1.3 %slice_bitcast_fusion = (f32[2,256]{1,0:T(2,128)}, f32[2,256]{1,0:T(2,128)}) fusion(f32[2,2,256]{2,1,0:T(2,128)} %gmres.1), kind=kLoop, calls=%fused_computation | loop fusion | bytes 8192 | tf_op jit(solution)/shard_map/squeeze | solution.py:469

commit v4 on v3

--- a/solution.py
+++ b/solution.py
@@ -440,7 +440,7 @@
     dma = pltpu.SemaphoreType.DMA
     out = pl.pallas_call(
         kernel,
-        out_shape=jax.ShapeDtypeStruct((2, *rhs.shape), F32),
+        out_shape=pltpu.VMEM((2, *rhs.shape), F32),
         in_specs=[hbm] * 10,
         out_specs=pl.BlockSpec(memory_space=pltpu.VMEM),
         scratch_shapes=[

time: 61.3 us -> 60 us (0.979)
  local copies, waits for them, and re-layouts: 1.26 us -> 0.59 us
    squeeze x1, local copies, waits for them, and re-layouts: 1.26 us -> 0.59 us  [shards(): return (out[0], out[1])]
where the time goes in v4:
time: 60 us; the launch traced here: 59.9 us
  Pallas kernels  58.6 us (98%)
  between operations  0.64 us (1%)
    pallas_call x1, Pallas kernels, shards(): pl.pallas_call(kernel, out_shape=pltpu.VMEM((2, *rhs.shape), F32), in_spe...  58.6 us

profile of v4, /device:TPU:1, one launch (start us, length us, event | category | flops | bytes accessed | tf_op | source)
XLA Modules:
  0.0 59.9 jit_solution(10824219747366053929)
XLA Ops:
  0.6 58.6 %gmres.1 = f32[2,2,256]{2,1,0:T(2,128)S(1)} custom-call(s32[8]{0:T(128)} %near_row_hbm.1, s32[8]{0:T(128)} %near_col_hbm.1, s32[6]{0:T(128)} %far_row_hbm.1, s32[6]{0:T(128)} %far_col_hbm.1, s32[6]{0:T(128)} %far_rank_hbm.1, f32[2,256]{1,0:T(2,128)} %rhs_hbm.1, f32[2,256]{1,0:T(2,128)} %self_hbm.1, bf16[8,256,256]{2,1,0:T(8,128)(2,1)} %near_hbm.1, ...), custom_call_target="tpu_custom_call" | custom-call | tf_op jit(solution)/shard_map/gmres/pallas_call | solution.py:441
  59.3 0.6 slice_bitcast_fusion

commit v5 on v4

--- a/solution.py
+++ b/solution.py
@@ -24,7 +24,7 @@
 
 
 RANKS = {i: ranked(signed(-i % 16)) for i in ALONG}
-OFFSETS = ((0, 0), (0, 1), (2, 0), (0, 3), (1, 0), (1, 1), (3, 0), (3, 1))
+OFFSETS = ((0, 0), (0, 1), (0, 2), (0, 3), (1, 0), (3, 3), (3, 0), (1, 3))
 BOUNDS = ((0, 4, 3), (4, 12, 8), (12, 20, 8))
 
 
@@ -267,15 +267,19 @@
         send(pair.at[stage, 0], pair.at[stage, 1], pair_send.at[stage], pair_recv.at[stage], sibling)
         sending(pair.at[stage, 0], pair_send.at[stage])
 
+    def spread(value):
+        return jnp.broadcast_to(value, (4, 128))
+
     def take_sums(stage, count):
         arrived(pair.at[stage, 1], pair_recv.at[stage])
         row = pair[stage, 0] + pair[stage, 1]
         if stage == 2:
             arrived(sums.at[stage, 0:14], sums_recv.at[stage, 1])
             row += jnp.sum(sums[stage, 9:23], axis=0)
-        return [row[:, n : n + 1] for n in range(count)]
-
-    for batch, (start, stop, count) in enumerate(BOUNDS):
+        return [spread(row[:, n : n + 1]) if stage == 2 else row[:, n : n + 1] for n in range(count)]
+
+    def along_batch(batch):
+        start, stop, count = BOUNDS[batch]
         arrived(along.at[0:count], along_recv.at[batch])
         for e in range(start, stop):
             flat_along[4 * e : 4 * e + 4] = along[e]
@@ -283,6 +287,7 @@
         own_tiles[0][batch][b] = part if batch == 0 else part.reshape(2, 16, 128)
         send_batch(0, batch)
 
+    along_batch(0)
     arrived(plane.at[0:15], plane_recv.at[0])
     index = jnp.zeros((4, 128), F32)
     for dev in range(16):
@@ -290,7 +295,10 @@
         flat_self[4 * dev : 4 * dev + 4] = plane[dev, 4:8]
         index += plane[dev, 8:12]
     squares = flat_rhs[...] * flat_rhs[...]
-    send_sums(0, [total(squares), total(squares * flat_self[...])])
+    squares_here, diagonal_here = total(squares), total(squares * flat_self[...])
+    along_batch(1)
+    along_batch(2)
+    send_sums(0, [squares_here, diagonal_here])
     index = index.astype(jnp.int32)
     spots = lax.broadcasted_iota(jnp.int32, (64, 256), 0) + 1
     selects = [
@@ -402,8 +410,9 @@
 
     own_first, own_basis, own_rest = mine_of(first), mine_of(basis), mine_of(rest)
     turn = 1.0 / radius
-    cosine = h11 * turn
-    sine = h21 * turn
+    cosine, sine, sine_beta, cosine_beta = h11 * turn, h21 * turn, h21 * turn * beta, h11 * turn * beta
+    turn, cosine, sine, sine_beta, cosine_beta = map(spread, (turn, cosine, sine, sine_beta, cosine_beta))
+    guess, g11 = spread(guess), spread(g11)
 
     @pl.when(even > 0)
     def _():
@@ -423,8 +432,8 @@
     square = jnp.maximum(square, 0.0) + 1e-06
     upper = cosine * h12 + sine * h22
     lower = cosine * h22 - sine * h12
-    coef_two = -(lower / (lower * lower + square)) * (sine * beta)
-    coef_one = (cosine * beta - upper * coef_two) * turn
+    coef_two = -(lower / (lower * lower + square)) * sine_beta
+    coef_one = (cosine_beta - upper * coef_two) * turn
 
     def wide(value):
         return jnp.concatenate([value[0:2], value[2:4]], axis=1)

time: 60 us -> 59.1 us (0.985)
  Pallas kernels: 58.6 us -> 57.7 us
    pallas_call x1, Pallas kernels: 58.6 us -> 57.7 us  [shards(): pl.pallas_call(kernel, out_shape=pltpu.VMEM((2, *rhs.shape), F32), in_spe...]
where the time goes in v5:
time: 59.1 us; the launch traced here: 59 us
  Pallas kernels  57.7 us (98%)
  between operations  0.64 us (1%)
    pallas_call x1, Pallas kernels, shards(): pl.pallas_call(kernel, out_shape=pltpu.VMEM((2, *rhs.shape), F32), in_spe...  57.7 us

profile of v5, /device:TPU:1, one launch (start us, length us, event | category | flops | bytes accessed | tf_op | source)
XLA Modules:
  0.0 59.0 jit_solution(17673207537830497257)
XLA Ops:
  0.6 57.7 %gmres.1 = f32[2,2,256]{2,1,0:T(2,128)S(1)} custom-call(s32[8]{0:T(128)} %near_row_hbm.1, s32[8]{0:T(128)} %near_col_hbm.1, s32[6]{0:T(128)} %far_row_hbm.1, s32[6]{0:T(128)} %far_col_hbm.1, s32[6]{0:T(128)} %far_rank_hbm.1, f32[2,256]{1,0:T(2,128)} %rhs_hbm.1, f32[2,256]{1,0:T(2,128)} %self_hbm.1, bf16[8,256,256]{2,1,0:T(8,128)(2,1)} %near_hbm.1, ...), custom_call_target="tpu_custom_call" | custom-call | tf_op jit(solution)/shard_map/gmres/pallas_call | solution.py:450
  58.4 0.6 slice_bitcast_fusion

commit v6 on v5

--- a/solution.py
+++ b/solution.py
@@ -217,8 +217,10 @@
     def joined(value):
         return jnp.concatenate([value[:16], value[16:]], axis=1)
 
-    def send_terms(it, kind, value):
+    def hold_terms(it, kind, value):
         terms[it, kind, b] = halves(value).astype(BF16)
+
+    def send_terms(it, kind):
         for j in PLANE:
             part = terms.at[it, kind, b]
             send(part, part, terms_send.at[it, kind], terms_recv.at[it, kind], (r, peer[j]))
@@ -295,7 +297,7 @@
         flat_self[4 * dev : 4 * dev + 4] = plane[dev, 4:8]
         index += plane[dev, 8:12]
     squares = flat_rhs[...] * flat_rhs[...]
-    squares_here, diagonal_here = total(squares), total(squares * flat_self[...])
+    squares_here, diagonal_here = total(squares), total(squares * (flat_self[...] * 0.125))
     along_batch(1)
     along_batch(2)
     send_sums(0, [squares_here, diagonal_here])
@@ -317,15 +319,17 @@
         if it == 0:
             for load in loads[7:]:
                 load.wait()
-        send_terms(it, 0, near_terms(picks))
+        hold_terms(it, 0, near_terms(picks))
         pick[...] = picks
         finish_batch(it, 1)
+        send_terms(it, 0)
         picks = pick[...] + picked(hot_middle[it, 0], own_tiles[it][1][...])
         arrived(other_tiles[it][1], core_recv.at[it, 1])
         picks += picked(hot_middle[it, 1], other_tiles[it][1][...])
         finish_batch(it, 2)
         picks += picked(hot_last[it], own_tiles[it][2][...])
-        send_terms(it, 1, far_terms(picks))
+        hold_terms(it, 1, far_terms(picks))
+        send_terms(it, 1)
         pair_sums(it)
         known = before(take_terms(it, 0, selects[0]))
         return known, take_terms(it, 1, selects[1])
@@ -333,7 +337,7 @@
     def before_1(sums_near):
         beta_squared, diagonal = take_sums(0, 2)
         beta = jnp.sqrt(beta_squared)
-        guess = diagonal / beta_squared
+        guess = 8.0 * (diagonal / beta_squared)
         inverse = 1.0 / beta
         first = flat_rhs[...] * inverse
         image = (flat_self[...] * flat_rhs[...] + sums_near) * inverse
@@ -375,7 +379,6 @@
     def _():
         first_2[0, 0, 0] = tile[quarter]
 
-    send_sums(1, [g11_here, total(first * shifted), total(shifted * shifted)])
 
     @pl.when(even > 0)
     def _():
@@ -383,6 +386,7 @@
 
     tile_copy(1).wait_recv()
     send_batch(1, 0)
+    send_sums(1, [g11_here, total(first * shifted), total(shifted * shifted)])
     arrived(middle_2.at[0, 0], tile_recv.at[2])
     send_batch(1, 1)
     arrived(last_2.at[0], tile_recv.at[3])

time: 59.1 us -> 59 us (level)
  no operation moved by 1% of the time
where the time goes in v6:
time: 59 us; the launch traced here: 58.9 us
  Pallas kernels  57.7 us (98%)
  between operations  0.64 us (1%)
  local copies, waits for them, and re-layouts  0.59 us (1%)
    pallas_call x1, Pallas kernels, shards(): pl.pallas_call(kernel, out_shape=pltpu.VMEM((2, *rhs.shape), F32), in_spe...  57.7 us

profile of v6, /device:TPU:1, one launch (start us, length us, event | category | flops | bytes accessed | tf_op | source)
XLA Modules:
  0.0 58.9 jit_solution(14658615079037984007)
XLA Ops:
  0.6 57.7 %gmres.1 = f32[2,2,256]{2,1,0:T(2,128)S(1)} custom-call(s32[8]{0:T(128)} %near_row_hbm.1, s32[8]{0:T(128)} %near_col_hbm.1, s32[6]{0:T(128)} %far_row_hbm.1, s32[6]{0:T(128)} %far_col_hbm.1, s32[6]{0:T(128)} %far_rank_hbm.1, f32[2,256]{1,0:T(2,128)} %rhs_hbm.1, f32[2,256]{1,0:T(2,128)} %self_hbm.1, bf16[8,256,256]{2,1,0:T(8,128)(2,1)} %near_hbm.1, ...), custom_call_target="tpu_custom_call" | custom-call | tf_op jit(solution)/shard_map/gmres/pallas_call | solution.py:454
  58.3 0.6 slice_bitcast_fusion
